TPU v7x, 32 devices: a whole 2x2x4 slice. The times are simulated.
32 devices in a mesh: groups: 2 (over y), blk: 4 (over z), dim: 4 (over x, core).
Axes of the slice: x: 2, y: 2, z: 4, core: 2. Of those that a mesh axis runs over, the one named last changes fastest.
Arguments:
- gradients: bfloat16 [2, 2816, 8192], P(None, ('groups', 'blk'), 'dim'), parts along dimension 1, may hold values from -0.65625 to 0.65625
- example_ids: int32 [2816], P(('groups', 'blk')), parts along dimension 0, may hold values from 0 to 1407
- lr_weights: float32 [2], replicated, may hold values from 0.3 to 3
- checkpoint_order: int32 [2], replicated, may hold values from 0 to 1, each once
Outputs:
- scores: float32 [2816, 1408], P(('groups', 'blk', 'dim')), parts along dimension 0
There are 2 independent parts, one for each index of `groups`. A program takes and returns all parts, laid end to end along the dimension named above; an argument that names none is the same for every part. Nothing has to cross between parts.
Inputs may be any that keep to these rules, and one draw needn't show every extreme that they name: `checkpoint_order`: each checkpoint index appears once.
All inputs are finite; a program needn't handle non-finite values.
Results may differ from a plain program's by a relative error of at most 0.008.
Values may be sent and summed in bfloat16 or wider, within the bound.
A program may use at most 64 MiB of HBM per device.

v0:
```python
import jax
import jax.numpy as jnp
from jax import lax
from jax.sharding import PartitionSpec as P


def passed_along(value, axis, steps):
    count = lax.axis_size(axis)
    pairs = [(source, (source + steps) % count) for source in range(count)]
    return lax.ppermute(value, axis, pairs)


def tile_term(local, remote, weights):
    products = lax.dot_general(
        local, remote, (((2,), (2,)), ((0,), (0,))), preferred_element_type=jnp.float32
    )
    return jnp.sum(weights[:, None, None] * products, axis=0).astype(jnp.bfloat16)


def place(totals, col_ids, block, ids, anchor, panel, nblk):
    start = jnp.mod(anchor, nblk) * panel
    totals = lax.dynamic_update_slice(totals, block, (jnp.int32(0), start))
    col_ids = lax.dynamic_update_slice(col_ids, ids.astype(jnp.int32), (start,))
    return (totals, col_ids)


def body(gradients, example_ids, lr_weights, checkpoint_order):
    slots = gradients.shape[0]
    panel = gradients.shape[1]
    nblk = lax.axis_size("blk")
    ndim = lax.axis_size("dim")
    rows = panel // ndim
    whole = panel * nblk
    slot_index = jnp.arange(slots, dtype=jnp.int32)
    weights = jnp.sum(
        jnp.where(
            checkpoint_order[:, None] == slot_index[None, :], lr_weights[None, :], jnp.float32(0.0)
        ),
        axis=1,
    )
    mine = lax.axis_index("blk")
    totals = jnp.zeros((rows, whole), jnp.float32)
    col_ids = jnp.zeros((whole,), jnp.int32)

    def direct(remote):
        return lax.psum_scatter(
            tile_term(gradients, remote, weights), "dim", scatter_dimension=0, tiled=True
        ).astype(jnp.float32)

    totals, col_ids = place(totals, col_ids, direct(gradients), example_ids, mine, panel, nblk)

    def advance(step, carry):
        current, current_ids, totals, col_ids = carry
        current, current_ids = passed_along((current, current_ids), "blk", 1)
        totals, col_ids = place(
            totals, col_ids, direct(current), current_ids, mine - step, panel, nblk
        )
        return (current, current_ids, totals, col_ids)

    carry = lax.fori_loop(1, nblk, advance, (gradients, example_ids, totals, col_ids))
    totals, col_ids = (carry[2], carry[3])
    row_ids = lax.dynamic_slice_in_dim(example_ids, lax.axis_index("dim") * rows, rows)
    same = row_ids[:, None] == col_ids[None, :]
    return jnp.where(same, jnp.float32(0.0), totals)


def solution(mesh):
    return jax.shard_map(
        body,
        mesh=mesh,
        in_specs=(P(None, ("groups", "blk"), "dim"), P(("groups", "blk")), P(), P()),
        out_specs=P(("groups", "blk", "dim"), None),
        check_vma=False,
    )
```

profile of v0, /device:TPU:0, one launch (start us, length us, event | category | flops | bytes accessed | tf_op | source)
XLA Modules:
  0.0 318.5 jit_solution(15247466099412536970)
XLA Ops:
  8.1 5.1 %fusion.1 = bf16[352,352]{1,0:T(8,128)(2,1)} fusion(bf16[2,352,2048]{2,1,0:T(8,128)(2,1)} %param.6, f32[2]{0:T(128)S(1)} %fusion.2), kind=kOutput, calls=%fused_computation.3 | convolution fusion | flops 1015393280 | bytes 3131400 | tf_op jit(solution)/shard_map/dot_general | solution.py:14
  13.3 3.8 %copy.10 = bf16[2,352,2048]{2,1,0:T(8,128)(2,1)} copy(bf16[2,352,2048]{2,1,0:T(8,128)(2,1)} %param.6) | data formatting | bytes 5767168
  17.3 18.6 %reduce-scatter.9.cloned.1.call-done = bf16[88,352]{1,0:T(8,128)(2,1)} async-done(((bf16[352,352]{1,0:T(8,128)(2,1)}), bf16[88,352]{1,0:T(8,128)(2,1)}) %reduce-scatter.9.cloned.1.call-update) | async-done | bytes 61968
  36.9 1.2 dynamic_update_slice.26
  38.1 273.1 %while.21 = (s32[]{:T(128)}, bf16[2,352,2048]{2,1,0:T(8,128)(2,1)}, s32[352]{0:T(512)S(1)}, f32[88,1408]{1,0:T(8,128)S(1)}, s32[1408]{0:T(1024)S(1)}, /*index=5*...) while((s32[]{:T(128)}, bf16[2,352,2048]{2,1,0:T(8,128)(2,1)}, ...), condition=%wide.region_6.7_spmd, body=%wide.region_3.6_spmd.sunk | while | flops 1015424256 | bytes 24719276 | solution.py:60
  38.1 1.7 collective-permute-start
  39.9 64.5 %collective-permute-done = bf16[2,352,2048]{2,1,0:T(8,128)(2,1)S(1)} collective-permute-done((bf16[2,352,2048]{2,1,0:T(8,128)(2,1)}, bf16[2,352,2048]{2,1,0:T(8,128)(2,1)S(1)}, u32[]{:S(2)}, u32[]{:S(2)}) %collective-permute-start) | collective-permute-done | bytes 2883616 | tf_op jit(solution)/shard_map/while/body/eval_jaxpr/ppermute | solution.py:10
  104.4 4.3 %fusion.12 = bf16[352,352]{1,0:T(8,128)(2,1)} fusion(bf16[2,352,2048]{2,1,0:T(8,128)(2,1)} %get-tuple-element.306, bf16[2,352,2048]{2,1,0:T(8,128)(2,1)S(1)} %collective-permute-done, f32[2]{0:T(128)S(1)} %get-tuple-element.305), kind=kOutput, calls=%fused_computation.1.clone.1 | convolution fusion | flops 1015393280 | bytes 6014984 | tf_op jit(solution)/shard_map/while/body/eval_jaxpr/dot_general | solution.py:14
  108.7 5.3 %collective-permute-done.1 = s32[352]{0:T(512)S(1)} collective-permute-done((s32[352]{0:T(512)S(1)}, s32[352]{0:T(512)S(1)}, u32[]{:S(2)}, u32[]{:S(2)}) %collective-permute-start.1) | collective-permute-done | bytes 1440 | tf_op jit(solution)/shard_map/while/body/eval_jaxpr/ppermute | solution.py:10
  114.3 1.6 copy.20
  115.8 10.8 %reduce-scatter.11.cloned.1.call-done = bf16[88,352]{1,0:T(8,128)(2,1)} async-done(((bf16[352,352]{1,0:T(8,128)(2,1)}), bf16[88,352]{1,0:T(8,128)(2,1)}) %reduce-scatter.11.cloned.1.call-update) | async-done | bytes 61968 | tf_op jit(solution)/shard_map/while
  128.5 1.8 collective-permute-start
  130.3 64.7 %collective-permute-done = bf16[2,352,2048]{2,1,0:T(8,128)(2,1)S(1)} collective-permute-done((bf16[2,352,2048]{2,1,0:T(8,128)(2,1)}, bf16[2,352,2048]{2,1,0:T(8,128)(2,1)S(1)}, u32[]{:S(2)}, u32[]{:S(2)}) %collective-permute-start) | collective-permute-done | bytes 2883616 | tf_op jit(solution)/shard_map/while/body/eval_jaxpr/ppermute | solution.py:10
  195.0 4.3 %fusion.12 = bf16[352,352]{1,0:T(8,128)(2,1)} fusion(bf16[2,352,2048]{2,1,0:T(8,128)(2,1)} %get-tuple-element.306, bf16[2,352,2048]{2,1,0:T(8,128)(2,1)S(1)} %collective-permute-done, f32[2]{0:T(128)S(1)} %get-tuple-element.305), kind=kOutput, calls=%fused_computation.1.clone.1 | convolution fusion | flops 1015393280 | bytes 6014984 | tf_op jit(solution)/shard_map/while/body/eval_jaxpr/dot_general | solution.py:14
  199.4 5.3 %collective-permute-done.1 = s32[352]{0:T(512)S(1)} collective-permute-done((s32[352]{0:T(512)S(1)}, s32[352]{0:T(512)S(1)}, u32[]{:S(2)}, u32[]{:S(2)}) %collective-permute-start.1) | collective-permute-done | bytes 1440 | tf_op jit(solution)/shard_map/while/body/eval_jaxpr/ppermute | solution.py:10
  204.9 1.6 copy.20
  206.5 11.2 %reduce-scatter.11.cloned.1.call-done = bf16[88,352]{1,0:T(8,128)(2,1)} async-done(((bf16[352,352]{1,0:T(8,128)(2,1)}), bf16[88,352]{1,0:T(8,128)(2,1)}) %reduce-scatter.11.cloned.1.call-update) | async-done | bytes 61968 | tf_op jit(solution)/shard_map/while
  218.6 1.4 dynamic_update_slice.30
  221.1 65.2 %collective-permute-done = bf16[2,352,2048]{2,1,0:T(8,128)(2,1)S(1)} collective-permute-done((bf16[2,352,2048]{2,1,0:T(8,128)(2,1)}, bf16[2,352,2048]{2,1,0:T(8,128)(2,1)S(1)}, u32[]{:S(2)}, u32[]{:S(2)}) %collective-permute-start) | collective-permute-done | bytes 2883616 | tf_op jit(solution)/shard_map/while/body/eval_jaxpr/ppermute | solution.py:10
  286.3 4.3 %fusion.12 = bf16[352,352]{1,0:T(8,128)(2,1)} fusion(bf16[2,352,2048]{2,1,0:T(8,128)(2,1)} %get-tuple-element.306, bf16[2,352,2048]{2,1,0:T(8,128)(2,1)S(1)} %collective-permute-done, f32[2]{0:T(128)S(1)} %get-tuple-element.305), kind=kOutput, calls=%fused_computation.1.clone.1 | convolution fusion | flops 1015393280 | bytes 6014984 | tf_op jit(solution)/shard_map/while/body/eval_jaxpr/dot_general | solution.py:14
  290.7 5.3 %collective-permute-done.1 = s32[352]{0:T(512)S(1)} collective-permute-done((s32[352]{0:T(512)S(1)}, s32[352]{0:T(512)S(1)}, u32[]{:S(2)}, u32[]{:S(2)}) %collective-permute-start.1) | collective-permute-done | bytes 1440 | tf_op jit(solution)/shard_map/while/body/eval_jaxpr/ppermute | solution.py:10
  296.2 1.6 copy.20
  297.8 11.0 %reduce-scatter.11.cloned.1.call-done = bf16[88,352]{1,0:T(8,128)(2,1)} async-done(((bf16[352,352]{1,0:T(8,128)(2,1)}), bf16[88,352]{1,0:T(8,128)(2,1)}) %reduce-scatter.11.cloned.1.call-update) | async-done | bytes 61968 | tf_op jit(solution)/shard_map/while
  309.7 1.4 dynamic_update_slice.30
  (30 shorter events, 9.1 us)
Async XLA Ops:
  6.5 29.4 %reduce-scatter.9.cloned.1.call-start = ((), (), s32[]{:S(2)}) async-start(), calls=%async_computation.2 | async-start | bytes 337920
  38.1 88.6 %reduce-scatter.11.cloned.1.call-start = ((), (), s32[]{:S(2)}) async-start(), calls=%async_computation.3 | async-start | bytes 337920 | tf_op jit(solution)/shard_map/while
  38.1 66.3 %collective-permute-start = (bf16[2,352,2048]{2,1,0:T(8,128)(2,1)}, bf16[2,352,2048]{2,1,0:T(8,128)(2,1)S(1)}, u32[]{:S(2)}, u32[]{:S(2)}) collective-permute-start(bf16[2,352,2048]{2,1,0:T(8,128)(2,1)} %get-tuple-element.287), channel_id=1, source_target_pairs={{0,4},{4,8},{8,12},{12,0},{1,5},{5,9},{9,13},{13,1},{2,6},{6,10},{... | collective-permute-start | bytes 8650760 | tf_op jit(solution)/shard_map/while/body/eval_jaxpr/ppermute | solution.py:10
  108.7 5.4 %collective-permute-start.1 = (s32[352]{0:T(512)S(1)}, s32[352]{0:T(512)S(1)}, u32[]{:S(2)}, u32[]{:S(2)}) collective-permute-start(s32[352]{0:T(512)S(1)} %get-tuple-element.288), channel_id=1, source_target_pairs={{0,4},{4,8},{8,12},{12,0},{1,5},{5,9},{9,13},{13,1},{2,6},{6,10},{... | collective-permute-start | bytes 4232 | tf_op jit(solution)/shard_map/while/body/eval_jaxpr/ppermute | solution.py:10
  128.4 89.3 %reduce-scatter.11.cloned.1.call-start = ((), (), s32[]{:S(2)}) async-start(), calls=%async_computation.3 | async-start | bytes 337920 | tf_op jit(solution)/shard_map/while
  128.5 66.5 %collective-permute-start = (bf16[2,352,2048]{2,1,0:T(8,128)(2,1)}, bf16[2,352,2048]{2,1,0:T(8,128)(2,1)S(1)}, u32[]{:S(2)}, u32[]{:S(2)}) collective-permute-start(bf16[2,352,2048]{2,1,0:T(8,128)(2,1)} %get-tuple-element.287), channel_id=1, source_target_pairs={{0,4},{4,8},{8,12},{12,0},{1,5},{5,9},{9,13},{13,1},{2,6},{6,10},{... | collective-permute-start | bytes 8650760 | tf_op jit(solution)/shard_map/while/body/eval_jaxpr/ppermute | solution.py:10
  199.3 5.4 %collective-permute-start.1 = (s32[352]{0:T(512)S(1)}, s32[352]{0:T(512)S(1)}, u32[]{:S(2)}, u32[]{:S(2)}) collective-permute-start(s32[352]{0:T(512)S(1)} %get-tuple-element.288), channel_id=1, source_target_pairs={{0,4},{4,8},{8,12},{12,0},{1,5},{5,9},{9,13},{13,1},{2,6},{6,10},{... | collective-permute-start | bytes 4232 | tf_op jit(solution)/shard_map/while/body/eval_jaxpr/ppermute | solution.py:10
  220.0 88.8 %reduce-scatter.11.cloned.1.call-start = ((), (), s32[]{:S(2)}) async-start(), calls=%async_computation.3 | async-start | bytes 337920 | tf_op jit(solution)/shard_map/while
  220.1 66.2 %collective-permute-start = (bf16[2,352,2048]{2,1,0:T(8,128)(2,1)}, bf16[2,352,2048]{2,1,0:T(8,128)(2,1)S(1)}, u32[]{:S(2)}, u32[]{:S(2)}) collective-permute-start(bf16[2,352,2048]{2,1,0:T(8,128)(2,1)} %get-tuple-element.287), channel_id=1, source_target_pairs={{0,4},{4,8},{8,12},{12,0},{1,5},{5,9},{9,13},{13,1},{2,6},{6,10},{... | collective-permute-start | bytes 8650760 | tf_op jit(solution)/shard_map/while/body/eval_jaxpr/ppermute | solution.py:10
  290.6 5.4 %collective-permute-start.1 = (s32[352]{0:T(512)S(1)}, s32[352]{0:T(512)S(1)}, u32[]{:S(2)}, u32[]{:S(2)}) collective-permute-start(s32[352]{0:T(512)S(1)} %get-tuple-element.288), channel_id=1, source_target_pairs={{0,4},{4,8},{8,12},{12,0},{1,5},{5,9},{9,13},{13,1},{2,6},{6,10},{... | collective-permute-start | bytes 4232 | tf_op jit(solution)/shard_map/while/body/eval_jaxpr/ppermute | solution.py:10
Sparse Core Ops, SparseCore 0:
  13.4 22.5 reduce-scatter.8
  108.8 17.7 reduce-scatter.10
  199.4 18.2 reduce-scatter.10
  290.7 18.0 reduce-scatter.10
where the time goes:
time: 319 us
  waiting for transfers between devices  262 us (82%)
  matrix products  17.9 us (6%)
  local copies, waits for them, and re-layouts  14.8 us (5%)
  between operations  13.1 us (4%)
  other arithmetic  5.3 us (2%)
  starting transfers between devices  4.9 us (2%)
    ppermute x6, waiting for transfers between devices, passed_along(): return lax.ppermute(value, axis, pairs)  210 us
    while x6, waiting for transfers between devices  33.1 us
    unnamed x2, waiting for transfers between devices  18.6 us
    dot_general x4, matrix products, tile_term(): lax.dot_general(local, remote, (((2,), (2,)), ((0,), (0,))), preferred_el...  17.9 us
  transfers between devices with their start and end apart: 10, of which 10 were waited for; matrix products, arithmetic and copies ran while one was open for 3% of the time, Pallas kernels for 0%

commit v1 on v0

--- a/solution.py
+++ b/solution.py
@@ -1,7 +1,13 @@
+import functools
+
 import jax
 import jax.numpy as jnp
 from jax import lax
+from jax.experimental import pallas as pl
+from jax.experimental.pallas import tpu as pltpu
 from jax.sharding import PartitionSpec as P
+
+F32, BF16 = jnp.float32, jnp.bfloat16
 
 
 def passed_along(value, axis, steps):
@@ -24,7 +30,7 @@
     return (totals, col_ids)
 
 
-def body(gradients, example_ids, lr_weights, checkpoint_order):
+def ring_body(gradients, example_ids, lr_weights, checkpoint_order):
     slots = gradients.shape[0]
     panel = gradients.shape[1]
     nblk = lax.axis_size("blk")
@@ -64,9 +70,211 @@
     return jnp.where(same, jnp.float32(0.0), totals)
 
 
+FA, FB, NEAR_T, NEAR_2, ID_N, ID_FA, ID_FB = range(7)
+CORE, CROSS, ZED = 7, 14, 21
+COPIES = 25
+T_FA, T_FB, T_N, T_B, DIAG, N_N, N_B = range(7)
+
+
+def dot_t(a, b):
+    return lax.dot_general(a, b, (((1,), (1,)), ((), ())), preferred_element_type=F32)
+
+
+def kernel(
+    g, ids, lr, order, out_d, out_n, out_f, out_ids,
+    gv, oside, fbuf, near2, idbuf,
+    acc_w, cs_w, cr_w, xs_w, xr_w, zs_w, zr_w,
+    acc_s, cs_s, cr_s, xs_s, xr_s, zs_s, zr_s,
+    send, recv, local,
+):
+    b, d = lax.axis_index("blk"), lax.axis_index("dim")
+    bp, ct = lax.rem(b, 2), b // 2
+    near = b + 1 - 2 * bp
+    fa, fb = lax.rem(b + 2, 4), lax.rem(near + 2, 4)
+    c, x = lax.rem(d, 2), d // 2
+    core, cross = d + 1 - 2 * c, lax.rem(d + 2, 4)
+    panel, feat = g.shape[1], g.shape[2]
+    half, rows = feat // 2, panel // 4
+
+    def cols(p):
+        return pl.ds(pl.multiple_of(p * half, 128), half)
+
+    loads = [
+        pltpu.make_async_copy(g, gv, local.at[0]),
+        pltpu.make_async_copy(g.at[ct, :, cols(bp)], oside.at[bp], local.at[1]),
+        pltpu.make_async_copy(ids, idbuf.at[b], local.at[2]),
+    ]
+    for load in loads:
+        load.start()
+
+    barrier = pltpu.get_barrier_semaphore()
+    for target in ({"blk": near}, {"blk": fa}, {"blk": fb}, {"dim": core}, {"dim": cross}):
+        pl.semaphore_signal(barrier, inc=1, device_id=target, device_id_type=pl.DeviceIdType.MESH)
+    pl.semaphore_wait(barrier, 5)
+
+    def remote(src, dst, k, target):
+        copy = pltpu.make_async_remote_copy(
+            src_ref=src, dst_ref=dst, send_sem=send.at[k], recv_sem=recv.at[k],
+            device_id=target, device_id_type=pl.DeviceIdType.MESH,
+        )
+        copy.start()
+        return copy
+
+    flight = {}
+    flight[FB] = remote(g.at[1 - ct, :, cols(1 - bp)], fbuf.at[bp], FB, {"blk": fb})
+    flight[FA] = remote(g.at[1 - ct, :, cols(bp)], fbuf.at[bp], FA, {"blk": fa})
+    flight[NEAR_T] = remote(g.at[ct, :, cols(1 - bp)], oside.at[bp], NEAR_T, {"blk": near})
+    flight[NEAR_2] = remote(g.at[1 - ct, :, cols(1 - bp)], near2, NEAR_2, {"blk": near})
+    for k, to in ((ID_N, near), (ID_FA, fa), (ID_FB, fb)):
+        flight[k] = remote(ids, idbuf.at[b], k, {"blk": to})
+
+    def weight(slot):
+        total = jnp.float32(0.0)
+        for k in range(lr.shape[0]):
+            total = total + jnp.where(order[slot] == k, lr[k], jnp.float32(0.0))
+        return total
+
+    w0, w1 = weight(0), weight(1)
+    w_t = jnp.where(ct == 0, w0, w1)
+    w_o = jnp.where(ct == 0, w1, w0)
+
+    def bufs(r):
+        if r < DIAG:
+            return r, acc_w, cs_w, cr_w, xs_w, xr_w
+        return r - DIAG, acc_s, cs_s, cr_s, xs_s, xr_s
+
+    def to_core(r, value):
+        i, acc, cs, cr, _, _ = bufs(r)
+        for q in range(4):
+            acc[i, q] = value[q * rows:(q + 1) * rows]
+        for q in range(2):
+            cs[i, q] = acc[i, 2 * q + 1 - c].astype(BF16)
+        flight[CORE + r] = remote(cs.at[i], cr.at[i], CORE + r, {"dim": core})
+
+    def to_cross(r):
+        i, acc, _, cr, xs, xr = bufs(r)
+        flight[CORE + r].wait_recv()
+        y = 1 - x
+        xs[i] = (acc[i, 2 * y + c] + cr[i, y].astype(F32)).astype(BF16)
+        flight[CROSS + r] = remote(xs.at[i], xr.at[i], CROSS + r, {"dim": cross})
+
+    def summed(r):
+        i, acc, _, cr, _, xr = bufs(r)
+        flight[CROSS + r].wait_recv()
+        return acc[i, 2 * x + c] + cr[i, x].astype(F32) + xr[i].astype(F32)
+
+    for load in loads:
+        load.wait()
+    to_core(DIAG, w0 * dot_t(gv[0], gv[0]) + w1 * dot_t(gv[1], gv[1]))
+    to_cross(DIAG)
+    out_d[...] = summed(DIAG)
+
+    flight[NEAR_T].wait_recv()
+    flight[NEAR_2].wait_recv()
+    own2 = gv[1 - ct, :, cols(bp)]
+    to_core(N_N, w_t * dot_t(oside[1 - bp], oside[bp]) + w_o * dot_t(near2[...], own2))
+    to_core(N_B, w_t * dot_t(oside[bp], oside[1 - bp]) + w_o * dot_t(own2, near2[...]))
+    to_cross(N_N)
+    to_cross(N_B)
+    zs_s[...] = summed(N_N).astype(BF16)
+    flight[ZED + 3] = remote(zs_s, zr_s, ZED + 3, {"blk": near})
+    n_own = summed(N_B)
+    flight[ZED + 3].wait_recv()
+    out_n[...] = n_own + zr_s[...].astype(F32)
+
+    flight[FA].wait_recv()
+    flight[FB].wait_recv()
+    side = oside[...].reshape(2 * panel, half)
+    far = fbuf[...].reshape(2 * panel, half)
+    to_core(T_FA, w_t * dot_t(fbuf[bp], side))
+    to_core(T_FB, w_t * dot_t(fbuf[1 - bp], side))
+    to_cross(T_FA)
+    to_core(T_N, w_t * dot_t(oside[1 - bp], far))
+    to_cross(T_FB)
+    to_core(T_B, w_t * dot_t(oside[bp], far))
+    to_cross(T_N)
+    to_cross(T_B)
+    for k, (r, to) in enumerate(((T_FA, fa), (T_FB, fb), (T_N, near))):
+        zs_w[k] = summed(r).astype(BF16)
+        flight[ZED + k] = remote(zs_w.at[k], zr_w.at[k], ZED + k, {"blk": to})
+    total = summed(T_B)
+    for k in (2, 0, 1):
+        flight[ZED + k].wait_recv()
+        total = total + zr_w[k].astype(F32)
+    out_f[...] = total
+    for k in (ID_N, ID_FA, ID_FB):
+        flight[k].wait_recv()
+    out_ids[...] = idbuf[...]
+    for k in range(COPIES):
+        flight[k].wait_send()
+
+
+def two_level_body(gradients, example_ids, lr_weights, checkpoint_order):
+    slots, panel, feat = gradients.shape
+    half, rows = feat // 2, panel // 4
+    vmem = pl.BlockSpec(memory_space=pltpu.VMEM)
+    smem = pl.BlockSpec(memory_space=pltpu.SMEM)
+
+    def partials(count, width):
+        return [
+            pltpu.VMEM((count, 4, rows, width), F32),
+            pltpu.VMEM((count, 2, rows, width), BF16),
+            pltpu.VMEM((count, 2, rows, width), BF16),
+            pltpu.VMEM((count, rows, width), BF16),
+            pltpu.VMEM((count, rows, width), BF16),
+        ]
+
+    d_tile, n_tile, f_tile, col_ids = pl.pallas_call(
+        kernel,
+        out_shape=[
+            jax.ShapeDtypeStruct((rows, panel), F32),
+            jax.ShapeDtypeStruct((rows, panel), F32),
+            jax.ShapeDtypeStruct((rows, 2 * panel), F32),
+            jax.ShapeDtypeStruct((4, 1, panel), jnp.int32),
+        ],
+        in_specs=[pl.BlockSpec(memory_space=pl.ANY), vmem, smem, smem],
+        out_specs=[vmem] * 4,
+        scratch_shapes=[
+            pltpu.VMEM((slots, panel, feat), BF16),
+            pltpu.VMEM((2, panel, half), BF16),
+            pltpu.VMEM((2, panel, half), BF16),
+            pltpu.VMEM((panel, half), BF16),
+            pltpu.VMEM((4, 1, panel), jnp.int32),
+            *partials(4, 2 * panel),
+            pltpu.VMEM((3, rows, 2 * panel), BF16),
+            pltpu.VMEM((3, rows, 2 * panel), BF16),
+            *partials(3, panel),
+            pltpu.VMEM((rows, panel), BF16),
+            pltpu.VMEM((rows, panel), BF16),
+            pltpu.SemaphoreType.DMA((COPIES,)),
+            pltpu.SemaphoreType.DMA((COPIES,)),
+            pltpu.SemaphoreType.DMA((3,)),
+        ],
+        compiler_params=pltpu.CompilerParams(
+            collective_id=0, has_side_effects=True, vmem_limit_bytes=48 * 1024 * 1024
+        ),
+    )(gradients, example_ids.reshape(1, panel), lr_weights, checkpoint_order)
+
+    b = lax.axis_index("blk")
+    side = jnp.where(
+        lax.rem(b, 2) == 0,
+        jnp.concatenate([d_tile, n_tile], axis=1),
+        jnp.concatenate([n_tile, d_tile], axis=1),
+    )
+    totals = jnp.where(
+        b < 2,
+        jnp.concatenate([side, f_tile], axis=1),
+        jnp.concatenate([f_tile, side], axis=1),
+    )
+    row_ids = lax.dynamic_slice_in_dim(example_ids, lax.axis_index("dim") * rows, rows)
+    same = row_ids[:, None] == col_ids.reshape(1, 4 * panel)
+    return jnp.where(same, jnp.float32(0.0), totals)
+
+
 def solution(mesh):
+    fits = mesh.shape["blk"] == 4 and mesh.shape["dim"] == 4
     return jax.shard_map(
-        body,
+        two_level_body if fits else ring_body,
         mesh=mesh,
         in_specs=(P(None, ("groups", "blk"), "dim"), P(("groups", "blk")), P(), P()),
         out_specs=P(("groups", "blk", "dim"), None),

time: 319 us -> 105 us (0.33)
  waiting for transfers between devices: 262 us -> 0 us
  Pallas kernels: 0 us -> 98.7 us
  matrix products: 17.9 us -> 0 us
  between operations: 13.1 us -> 0.02 us
  local copies, waits for them, and re-layouts: 14.8 us -> 4.64 us
  starting transfers between devices: 4.9 us -> 0 us
  other arithmetic: 5.3 us -> 1.2 us
    ppermute x6 -> x0, waiting for transfers between devices: 210 us -> none  [passed_along(): return lax.ppermute(value, axis, pairs)]
    pallas_call x0 -> x1, Pallas kernels: none -> 98.7 us  [two_level_body(): pl.pallas_call(kernel, out_shape=[jax.ShapeDtypeStruct((rows, panel), F32...]
    while x6 -> x0, waiting for transfers between devices: 33.1 us -> none
    unnamed x2 -> x0, waiting for transfers between devices: 18.6 us -> none
    dot_general x4 -> x0, matrix products: 17.9 us -> none  [tile_term(): lax.dot_general(local, remote, (((2,), (2,)), ((0,), (0,))), preferred_el...]
    dynamic_update_slice x8 -> x0, local copies, waits for them, and re-layouts: 5.55 us -> none  [the longest x4 4.81 us: place(): totals = lax.dynamic_update_slice(totals, block, (jnp.int32(0), start))]
    ppermute x6 -> x0, starting transfers between devices: 4.78 us -> none  [passed_along(): return lax.ppermute(value, axis, pairs)]
    while x6 -> x0, local copies, waits for them, and re-layouts: 4.74 us -> none
  transfers between devices with their start and end apart: 10 -> 0, of which waited for: 10 -> 0; matrix products, arithmetic and copies ran while one was open for 3% -> 0% of each run, Pallas kernels for 0% -> 0%
where the time goes in v1:
time: 105 us
  Pallas kernels  98.7 us (94%)
  local copies, waits for them, and re-layouts  4.64 us (4%)
  other arithmetic  1.2 us (1%)
    pallas_call x1, Pallas kernels, two_level_body(): pl.pallas_call(kernel, out_shape=[jax.ShapeDtypeStruct((rows, panel), F32...  98.7 us
    unnamed x6, local copies, waits for them, and re-layouts  3.12 us

profile of v1, /device:TPU:0, one launch (start us, length us, event | category | flops | bytes accessed | tf_op | source)
XLA Modules:
  0.0 104.5 jit_solution(7773486767207543215)
XLA Ops:
  0.0 0.8 dynamic_slice.3
  0.8 0.7 reshape.6.ids
  1.4 0.0 copy-start
  1.4 1.8 %copy-done = bf16[2,352,2048]{2,1,0:T(8,128)(2,1)S(1)} copy-done((bf16[2,352,2048]{2,1,0:T(8,128)(2,1)S(1)}, bf16[2,352,2048]{2,1,0:T(8,128)(2,1)}, u32[]{:S(2)}) %copy-start) | copy-done | bytes 2883608
  3.3 0.0 copy-start.1
  3.3 0.7 copy-done.1
  3.9 0.0 copy-start.2
  3.9 0.7 copy-done.2
  4.6 98.7 %shard_map.46 = (f32[88,352]{1,0:T(8,128)S(1)}, f32[88,352]{1,0:T(8,128)S(1)}, f32[88,704]{1,0:T(8,128)S(1)}, s32[4,1,352]{2,1,0:T(1,128)S(1)}) custom-call(bf16[2,352,2048]{2,1,0:T(8,128)(2,1)S(1)} %copy-done, s32[1,352]{1,0:T(1,128)S(1)} %reshape.6.ids, f32[2]{0:T(128)S(1)} %copy-done.1, s32[2]{0:T(128)S(1)} %copy-done.2), custom_call_target="tpu_custom_call" | custom-call | tf_op jit(solution)/shard_map/pallas_call | solution.py:227
  103.3 0.1 eq.19
  103.3 0.2 maximum_select_fusion.1
  103.5 1.0 fusion
  (1 shorter events, 0.0 us)
Async XLA Ops:
  1.4 1.8 %copy-start = (bf16[2,352,2048]{2,1,0:T(8,128)(2,1)S(1)}, bf16[2,352,2048]{2,1,0:T(8,128)(2,1)}, u32[]{:S(2)}) copy-start(bf16[2,352,2048]{2,1,0:T(8,128)(2,1)} %g.1) | copy-start | bytes 8650756
  3.3 0.7 copy-start.1
  3.9 0.7 copy-start.2

commit v2 on v1

v2 whole, which is shorter than its diff:
```python
import functools

import jax
import jax.numpy as jnp
from jax import lax
from jax.experimental import pallas as pl
from jax.experimental.pallas import tpu as pltpu
from jax.sharding import PartitionSpec as P

F32, BF16 = jnp.float32, jnp.bfloat16


def passed_along(value, axis, steps):
    count = lax.axis_size(axis)
    pairs = [(source, (source + steps) % count) for source in range(count)]
    return lax.ppermute(value, axis, pairs)


def tile_term(local, remote, weights):
    products = lax.dot_general(
        local, remote, (((2,), (2,)), ((0,), (0,))), preferred_element_type=jnp.float32
    )
    return jnp.sum(weights[:, None, None] * products, axis=0).astype(jnp.bfloat16)


def place(totals, col_ids, block, ids, anchor, panel, nblk):
    start = jnp.mod(anchor, nblk) * panel
    totals = lax.dynamic_update_slice(totals, block, (jnp.int32(0), start))
    col_ids = lax.dynamic_update_slice(col_ids, ids.astype(jnp.int32), (start,))
    return (totals, col_ids)


def ring_body(gradients, example_ids, lr_weights, checkpoint_order):
    slots = gradients.shape[0]
    panel = gradients.shape[1]
    nblk = lax.axis_size("blk")
    ndim = lax.axis_size("dim")
    rows = panel // ndim
    whole = panel * nblk
    slot_index = jnp.arange(slots, dtype=jnp.int32)
    weights = jnp.sum(
        jnp.where(
            checkpoint_order[:, None] == slot_index[None, :], lr_weights[None, :], jnp.float32(0.0)
        ),
        axis=1,
    )
    mine = lax.axis_index("blk")
    totals = jnp.zeros((rows, whole), jnp.float32)
    col_ids = jnp.zeros((whole,), jnp.int32)

    def direct(remote):
        return lax.psum_scatter(
            tile_term(gradients, remote, weights), "dim", scatter_dimension=0, tiled=True
        ).astype(jnp.float32)

    totals, col_ids = place(totals, col_ids, direct(gradients), example_ids, mine, panel, nblk)

    def advance(step, carry):
        current, current_ids, totals, col_ids = carry
        current, current_ids = passed_along((current, current_ids), "blk", 1)
        totals, col_ids = place(
            totals, col_ids, direct(current), current_ids, mine - step, panel, nblk
        )
        return (current, current_ids, totals, col_ids)

    carry = lax.fori_loop(1, nblk, advance, (gradients, example_ids, totals, col_ids))
    totals, col_ids = (carry[2], carry[3])
    row_ids = lax.dynamic_slice_in_dim(example_ids, lax.axis_index("dim") * rows, rows)
    same = row_ids[:, None] == col_ids[None, :]
    return jnp.where(same, jnp.float32(0.0), totals)


BOUNDS = (40,)
COPIES = 96


def far_chunks(rows):
    chunks, outer = [], rows
    for inner in (*BOUNDS, 0):
        ranges = []
        for pair in range(2):
            middle = (2 * pair + 1) * rows
            if inner:
                ranges += [(middle - outer, middle - inner), (middle + inner, middle + outer)]
            else:
                ranges += [(middle - outer, middle + outer)]
        merged = []
        for low, high in ranges:
            if merged and merged[-1][1] == low:
                merged[-1] = (merged[-1][0], high)
            else:
                merged.append((low, high))
        chunks.append((outer - inner, merged))
        outer = inner
    return chunks


def dot_t(a, b):
    return lax.dot_general(a, b, (((1,), (1,)), ((), ())), preferred_element_type=F32)


def kernel(
    g, ids, lr_in, order_in, out_d, out_n, out_f, out_ids,
    lr, order, gv, oside, near2, idbuf, send, recv, local, *scratch,
):
    b, d = lax.axis_index("blk"), lax.axis_index("dim")
    bp, ct = lax.rem(b, 2), b // 2
    near = b + 1 - 2 * bp
    fa, fb = lax.rem(b + 2, 4), lax.rem(near + 2, 4)
    c, x = lax.rem(d, 2), d // 2
    core, cross = d + 1 - 2 * c, lax.rem(d + 2, 4)
    panel, feat = g.shape[1], g.shape[2]
    half, rows = feat // 2, panel // 4
    chunks = far_chunks(rows)
    groups = [scratch[7 * k:7 * k + 7] for k in range(2 + 2 * len(chunks))]
    fbufs = scratch[7 * len(groups):]

    def cols(p):
        return pl.ds(pl.multiple_of(p * half, 128), half)

    loads = [
        pltpu.make_async_copy(g, gv, local.at[0]),
        pltpu.make_async_copy(g.at[ct, :, cols(bp)], oside.at[bp], local.at[1]),
        pltpu.make_async_copy(ids, idbuf.at[b], local.at[2]),
        pltpu.make_async_copy(lr_in, lr, local.at[3]),
        pltpu.make_async_copy(order_in, order, local.at[4]),
    ]

    barrier = pltpu.get_barrier_semaphore()
    for target in ({"blk": near}, {"blk": fa}, {"blk": fb}, {"dim": core}, {"dim": cross}):
        pl.semaphore_signal(barrier, inc=1, device_id=target, device_id_type=pl.DeviceIdType.MESH)
    pl.semaphore_wait(barrier, 5)

    started = []

    def remote(src, dst, target):
        k = len(started)
        copy = pltpu.make_async_remote_copy(
            src_ref=src, dst_ref=dst, send_sem=send.at[k], recv_sem=recv.at[k],
            device_id=target, device_id_type=pl.DeviceIdType.MESH,
        )
        copy.start()
        started.append(copy)
        return copy

    arriving = []

    def send_far(h):
        count, ranges = chunks[h]
        flight = []
        for to, p in ((fb, 1 - bp), (fa, bp)):
            place_at = 0
            for low, high in ranges:
                flight.append(remote(
                    g.at[1 - ct, pl.ds(low, high - low), cols(p)],
                    fbufs[h].at[bp, pl.ds(place_at, high - low)],
                    {"blk": to},
                ))
                place_at += high - low
        arriving.append(flight)

    send_far(0)
    near_t = remote(g.at[ct, :, cols(1 - bp)], oside.at[bp], {"blk": near})
    for load in loads:
        load.start()
    for load in loads:
        load.wait()
    id_copies = [remote(idbuf.at[b], idbuf.at[b], {"blk": to}) for to in (near, fa, fb)]

    def weight(slot):
        total = jnp.float32(0.0)
        for k in range(lr.shape[0]):
            total = total + jnp.where(order[slot] == k, lr[k], jnp.float32(0.0))
        return total

    w0, w1 = weight(0), weight(1)
    w_t = jnp.where(ct == 0, w0, w1)
    w_o = jnp.where(ct == 0, w1, w0)
    flight = {}

    def to_core(grp, i, value):
        acc, cs, cr = groups[grp][:3]
        height = acc.shape[2]
        for q in range(4):
            acc[i, q] = value[q * height:(q + 1) * height]
        for q in range(2):
            cs[i, q] = acc[i, 2 * q + 1 - c].astype(BF16)
        flight[grp, i, 0] = remote(cs.at[i], cr.at[i], {"dim": core})

    def to_cross(grp, i):
        acc, _, cr, xs, xr = groups[grp][:5]
        flight[grp, i, 0].wait_recv()
        y = 1 - x
        xs[i] = (acc[i, 2 * y + c] + cr[i, y].astype(F32)).astype(BF16)
        flight[grp, i, 1] = remote(xs.at[i], xr.at[i], {"dim": cross})

    def summed(grp, i):
        acc, _, cr, _, xr = groups[grp][:5]
        flight[grp, i, 1].wait_recv()
        return acc[i, 2 * x + c] + cr[i, x].astype(F32) + xr[i].astype(F32)

    def to_zed(grp, i, to):
        zs, zr = groups[grp][5:]
        zs[i] = summed(grp, i).astype(BF16)
        flight[grp, i, 2] = remote(zs.at[i], zr.at[i], {"blk": to})

    def arrived(grp, i):
        flight[grp, i, 2].wait_recv()
        return groups[grp][6][i].astype(F32)

    to_core(0, 0, w0 * dot_t(gv[0], gv[0]) + w1 * dot_t(gv[1], gv[1]))
    to_cross(0, 0)
    out_d[...] = summed(0, 0)

    def near_tiles():
        near_o.wait_recv()
        own2 = gv[1 - ct, :, cols(bp)]
        to_core(1, 0, w_t * dot_t(oside[1 - bp], oside[bp]) + w_o * dot_t(near2[...], own2))
        to_core(1, 1, w_t * dot_t(oside[bp], oside[1 - bp]) + w_o * dot_t(own2, near2[...]))
    def far_tiles(h):
        rowwise, colwise = 2 + 2 * h, 3 + 2 * h
        for copy in arriving[h]:
            copy.wait_recv()
        side = oside[...].reshape(2 * panel, half)
        far = fbufs[h][...].reshape(2 * fbufs[h].shape[1], half)
        last = h == len(chunks) - 1
        to_core(rowwise, 0, w_t * dot_t(fbufs[h][bp], side))
        to_core(rowwise, 1, w_t * dot_t(fbufs[h][1 - bp], side))
        to_cross(rowwise, 0)
        to_core(colwise, 0, w_t * dot_t(oside[1 - bp], far))
        to_cross(rowwise, 1)
        to_core(colwise, 1, w_t * dot_t(oside[bp], far))
        to_cross(colwise, 0)
        to_zed(rowwise, 0, fa)
        to_cross(colwise, 1)
        to_zed(rowwise, 1, fb)
        if last:
            near_tiles()
        to_zed(colwise, 0, near)
        if last:
            to_cross(1, 0)
            to_cross(1, 1)
            to_zed(1, 0, near)

    def finish_cols(h):
        own = summed(3 + 2 * h, 1) + arrived(3 + 2 * h, 0)
        at = 0
        for p in range(2):
            for low, high in chunks[h][1]:
                out_f[:, p * panel + low:p * panel + high] = own[:, at:at + high - low]
                at += high - low

    def finish_rows(h):
        count = chunks[h][0]
        before = sum(chunk[0] for chunk in chunks[:h])
        at = jnp.where(c == 0, before, rows - before - count)
        at = pl.multiple_of(at, 8)
        out_f[pl.ds(at, count)] = out_f[pl.ds(at, count)] + arrived(2 + 2 * h, 0) + arrived(2 + 2 * h, 1)

    near_t.wait_recv()
    left = [near_t]
    for h in range(len(chunks)):
        if h == 0:
            near_t.wait_send()
        if h + 1 < len(chunks):
            for copy in arriving[h]:
                copy.wait_send()
            left += arriving[h]
            if h == 0:
                near_o = remote(g.at[1 - ct, :, cols(1 - bp)], near2, {"blk": near})
            send_far(h + 1)
        if h > 0:
            finish_cols(h - 1)
        far_tiles(h)
    finish_cols(len(chunks) - 1)
    for h in range(len(chunks)):
        finish_rows(h)
    out_n[...] = summed(1, 1) + arrived(1, 0)
    for copy in id_copies:
        copy.wait_recv()
    out_ids[...] = idbuf[...]
    for copy in started:
        if not any(copy is other for other in left):
            copy.wait_send()


def two_level_body(gradients, example_ids, lr_weights, checkpoint_order):
    slots, panel, feat = gradients.shape
    half, rows = feat // 2, panel // 4
    vmem = pl.BlockSpec(memory_space=pltpu.VMEM)
    anywhere = pl.BlockSpec(memory_space=pl.ANY)
    chunks = far_chunks(rows)

    def partials(count, height, width):
        return [
            pltpu.VMEM((count, 4, height, width), F32),
            pltpu.VMEM((count, 2, height, width), BF16),
            pltpu.VMEM((count, 2, height, width), BF16),
            *[pltpu.VMEM((count, height, width), BF16)] * 4,
        ]

    scratch = partials(1, rows, panel) + partials(2, rows, panel)
    for count, _ in chunks:
        scratch += partials(2, count, 2 * panel) + partials(2, rows, 8 * count)
    scratch += [pltpu.VMEM((2, 4 * count, half), BF16) for count, _ in chunks]

    d_tile, n_tile, f_tile, col_ids = pl.pallas_call(
        kernel,
        out_shape=[
            jax.ShapeDtypeStruct((rows, panel), F32),
            jax.ShapeDtypeStruct((rows, panel), F32),
            jax.ShapeDtypeStruct((rows, 2 * panel), F32),
            jax.ShapeDtypeStruct((4, 1, panel), jnp.int32),
        ],
        in_specs=[anywhere] * 4,
        out_specs=[vmem] * 4,
        scratch_shapes=[
            pltpu.SMEM(lr_weights.shape, F32),
            pltpu.SMEM(checkpoint_order.shape, jnp.int32),
            pltpu.VMEM((slots, panel, feat), BF16),
            pltpu.VMEM((2, panel, half), BF16),
            pltpu.VMEM((panel, half), BF16),
            pltpu.VMEM((4, 1, panel), jnp.int32),
            pltpu.SemaphoreType.DMA((COPIES,)),
            pltpu.SemaphoreType.DMA((COPIES,)),
            pltpu.SemaphoreType.DMA((5,)),
            *scratch,
        ],
        compiler_params=pltpu.CompilerParams(
            collective_id=0, has_side_effects=True, vmem_limit_bytes=60 * 1024 * 1024
        ),
    )(gradients, example_ids.reshape(1, panel), lr_weights, checkpoint_order)

    b = lax.axis_index("blk")
    side = jnp.where(
        lax.rem(b, 2) == 0,
        jnp.concatenate([d_tile, n_tile], axis=1),
        jnp.concatenate([n_tile, d_tile], axis=1),
    )
    totals = jnp.where(
        b < 2,
        jnp.concatenate([side, f_tile], axis=1),
        jnp.concatenate([f_tile, side], axis=1),
    )
    row_ids = lax.dynamic_slice_in_dim(example_ids, lax.axis_index("dim") * rows, rows)
    same = row_ids[:, None] == col_ids.reshape(1, 4 * panel)
    return jnp.where(same, jnp.float32(0.0), totals)


def solution(mesh):
    fits = mesh.shape["blk"] == 4 and mesh.shape["dim"] == 4
    return jax.shard_map(
        two_level_body if fits else ring_body,
        mesh=mesh,
        in_specs=(P(None, ("groups", "blk"), "dim"), P(("groups", "blk")), P(), P()),
        out_specs=P(("groups", "blk", "dim"), None),
        check_vma=False,
    )
```

time: 105 us -> 98.3 us (0.936)
  Pallas kernels: 98.7 us -> 92 us
  other arithmetic: 1.2 us -> 4.03 us
  local copies, waits for them, and re-layouts: 4.64 us -> 2.08 us
    pallas_call x1, Pallas kernels: 98.7 us -> 92 us  [two_level_body(): pl.pallas_call(kernel, out_shape=[jax.ShapeDtypeStruct((rows, panel), F32...]
    unnamed x6 -> x0, local copies, waits for them, and re-layouts: 3.12 us -> none
    select_n x1, other arithmetic: 0.16 us -> 1.27 us  [two_level_body(): jnp.where(lax.rem(b, 2) == 0, jnp.concatenate([d_tile, n_tile], axis=1),...]
where the time goes in v2:
time: 98.3 us; the launch traced here: 98.1 us
  Pallas kernels  92 us (94%)
  other arithmetic  4.03 us (4%)
  local copies, waits for them, and re-layouts  2.08 us (2%)
    pallas_call x1, Pallas kernels, two_level_body(): pl.pallas_call(kernel, out_shape=[jax.ShapeDtypeStruct((rows, panel), F32...  92 us
    select_n x1, other arithmetic, two_level_body(): return jnp.where(same, jnp.float32(0.0), totals)  2.04 us

profile of v2, /device:TPU:0, one launch (start us, length us, event | category | flops | bytes accessed | tf_op | source)
XLA Modules:
  0.0 98.1 jit_solution(16679817227728074781)
XLA Ops:
  0.0 0.8 dynamic_slice.3
  0.8 1.2 %reshape.6.ids = s32[1,352]{1,0:T(1,128)} reshape(s32[352]{0:T(512)} %param.5) | data formatting | bytes 2816 | tf_op jit(solution)/shard_map/reshape | solution.py:332
  2.0 92.0 %shard_map.46 = (f32[88,352]{1,0:T(8,128)}, f32[88,352]{1,0:T(8,128)}, f32[88,704]{1,0:T(8,128)}, s32[4,1,352]{2,1,0:T(1,128)}) custom-call(bf16[2,352,2048]{2,1,0:T(8,128)(2,1)} %g.1, s32[1,352]{1,0:T(1,128)} %reshape.6.ids, f32[2]{0:T(128)} %lr_in.1, s32[2]{0:T(128)} %order_in.1), custom_call_target="tpu_custom_call" | custom-call | tf_op jit(solution)/shard_map/pallas_call | solution.py:307
  94.0 0.7 reduce
  94.7 0.1 eq.19
  94.8 1.3 %maximum_select_fusion.1 = f32[88,704]{1,0:T(8,128)S(1)} fusion(f32[88,352]{1,0:T(8,128)} %get-tuple-element.11, f32[88,352]{1,0:T(8,128)} %get-tuple-element.10, pred[]{:T(512)S(6)} %eq.22), kind=kLoop, calls=%fused_computation.2 | loop fusion | flops 185856 | bytes 495617 | tf_op jit(solution)/shard_map/jit(_where)/select_n | solution.py:335
  96.1 2.0 %fusion = f32[88,1408]{1,0:T(8,128)} fusion(f32[88,704]{1,0:T(8,128)} %get-tuple-element.12, f32[88,704]{1,0:T(8,128)S(1)} %maximum_select_fusion.1, s32[1408]{0:T(1024)S(1)} %eq.19, s32[88]{0:T(128)S(1)} %dynamic_slice.3, pred[]{:T(512)S(6)} %lt.7), kind=kLoop, calls=%fused_computation.1 | loop fusion | flops 619520 | bytes 997217 | tf_op jit(solution)/shard_map/jit(_where)/select_n | solution.py:347

commit v3 on v2

--- a/solution.py
+++ b/solution.py
@@ -70,7 +70,9 @@
     return jnp.where(same, jnp.float32(0.0), totals)
 
 
-BOUNDS = (40,)
+BOUNDS = (24,)
+EARLY = True
+PACE = 1
 COPIES = 96
 
 
@@ -161,6 +163,14 @@
 
     send_far(0)
     near_t = remote(g.at[ct, :, cols(1 - bp)], oside.at[bp], {"blk": near})
+    near_o = []
+
+    def send_near(part):
+        piece = pl.ds(part * 2 * rows, 2 * rows)
+        near_o.append(remote(g.at[1 - ct, piece, cols(1 - bp)], near2.at[piece], {"blk": near}))
+
+    if EARLY:
+        send_near(0)
     for load in loads:
         load.start()
     for load in loads:
@@ -209,11 +219,10 @@
         return groups[grp][6][i].astype(F32)
 
     to_core(0, 0, w0 * dot_t(gv[0], gv[0]) + w1 * dot_t(gv[1], gv[1]))
-    to_cross(0, 0)
-    out_d[...] = summed(0, 0)
 
     def near_tiles():
-        near_o.wait_recv()
+        for copy in near_o:
+            copy.wait_recv()
         own2 = gv[1 - ct, :, cols(bp)]
         to_core(1, 0, w_t * dot_t(oside[1 - bp], oside[bp]) + w_o * dot_t(near2[...], own2))
         to_core(1, 1, w_t * dot_t(oside[bp], oside[1 - bp]) + w_o * dot_t(own2, near2[...]))
@@ -263,16 +272,21 @@
         if h == 0:
             near_t.wait_send()
         if h + 1 < len(chunks):
-            for copy in arriving[h]:
-                copy.wait_send()
-            left += arriving[h]
+            widths = [high - low for low, high in chunks[h][1]] * 2
+            for copy, width in zip(arriving[h], widths):
+                if PACE == 0 or (PACE == 1 and width < max(widths)):
+                    copy.wait_send()
+                    left.append(copy)
             if h == 0:
-                near_o = remote(g.at[1 - ct, :, cols(1 - bp)], near2, {"blk": near})
+                for part in range(len(near_o), 2):
+                    send_near(part)
             send_far(h + 1)
-        if h > 0:
-            finish_cols(h - 1)
+        if h == 0:
+            to_cross(0, 0)
         far_tiles(h)
-    finish_cols(len(chunks) - 1)
+    out_d[...] = summed(0, 0)
+    for h in range(len(chunks)):
+        finish_cols(h)
     for h in range(len(chunks)):
         finish_rows(h)
     out_n[...] = summed(1, 1) + arrived(1, 0)

time: 98.3 us -> 95.6 us (0.973)
  Pallas kernels: 92 us -> 88.8 us
    pallas_call x1, Pallas kernels: 92 us -> 88.8 us  [two_level_body(): pl.pallas_call(kernel, out_shape=[jax.ShapeDtypeStruct((rows, panel), F32...]
where the time goes in v3:
time: 95.6 us; the launch traced here: 94.9 us
  Pallas kernels  88.8 us (93%)
  other arithmetic  4.03 us (4%)
  local copies, waits for them, and re-layouts  2.08 us (2%)
    pallas_call x1, Pallas kernels, two_level_body(): pl.pallas_call(kernel, out_shape=[jax.ShapeDtypeStruct((rows, panel), F32...  88.8 us
    select_n x1, other arithmetic, two_level_body(): return jnp.where(same, jnp.float32(0.0), totals)  2.04 us

profile of v3, /device:TPU:0, one launch (start us, length us, event | category | flops | bytes accessed | tf_op | source)
XLA Modules:
  0.0 94.9 jit_solution(8821525593647066318)
XLA Ops:
  0.0 0.8 dynamic_slice.3
  0.8 1.2 %reshape.6.ids = s32[1,352]{1,0:T(1,128)} reshape(s32[352]{0:T(512)} %param.5) | data formatting | bytes 2816 | tf_op jit(solution)/shard_map/reshape | solution.py:346
  2.0 88.8 %shard_map.46 = (f32[88,352]{1,0:T(8,128)}, f32[88,352]{1,0:T(8,128)}, f32[88,704]{1,0:T(8,128)}, s32[4,1,352]{2,1,0:T(1,128)}) custom-call(bf16[2,352,2048]{2,1,0:T(8,128)(2,1)} %g.1, s32[1,352]{1,0:T(1,128)} %reshape.6.ids, f32[2]{0:T(128)} %lr_in.1, s32[2]{0:T(128)} %order_in.1), custom_call_target="tpu_custom_call" | custom-call | tf_op jit(solution)/shard_map/pallas_call | solution.py:321
  90.8 0.7 reduce
  91.5 0.1 eq.19
  91.6 1.3 %maximum_select_fusion.1 = f32[88,704]{1,0:T(8,128)S(1)} fusion(f32[88,352]{1,0:T(8,128)} %get-tuple-element.11, f32[88,352]{1,0:T(8,128)} %get-tuple-element.10, pred[]{:T(512)S(6)} %eq.22), kind=kLoop, calls=%fused_computation.2 | loop fusion | flops 185856 | bytes 495617 | tf_op jit(solution)/shard_map/jit(_where)/select_n | solution.py:349
  92.8 2.0 %fusion = f32[88,1408]{1,0:T(8,128)} fusion(f32[88,704]{1,0:T(8,128)} %get-tuple-element.12, f32[88,704]{1,0:T(8,128)S(1)} %maximum_select_fusion.1, s32[1408]{0:T(1024)S(1)} %eq.19, s32[88]{0:T(128)S(1)} %dynamic_slice.3, pred[]{:T(512)S(6)} %lt.7), kind=kLoop, calls=%fused_computation.1 | loop fusion | flops 619520 | bytes 997217 | tf_op jit(solution)/shard_map/jit(_where)/select_n | solution.py:361

commit v4 on v3

--- a/solution.py
+++ b/solution.py
@@ -171,6 +171,7 @@
 
     if EARLY:
         send_near(0)
+        send_near(1)
     for load in loads:
         load.start()
     for load in loads:
@@ -243,13 +244,7 @@
         to_zed(rowwise, 0, fa)
         to_cross(colwise, 1)
         to_zed(rowwise, 1, fb)
-        if last:
-            near_tiles()
         to_zed(colwise, 0, near)
-        if last:
-            to_cross(1, 0)
-            to_cross(1, 1)
-            to_zed(1, 0, near)
 
     def finish_cols(h):
         own = summed(3 + 2 * h, 1) + arrived(3 + 2 * h, 0)
@@ -283,6 +278,11 @@
             send_far(h + 1)
         if h == 0:
             to_cross(0, 0)
+        if h == len(chunks) - 1:
+            near_tiles()
+            to_cross(1, 0)
+            to_cross(1, 1)
+            to_zed(1, 0, near)
         far_tiles(h)
     out_d[...] = summed(0, 0)
     for h in range(len(chunks)):

time: 95.6 us -> 94.5 us (0.988)
  no operation moved by 1% of the time
where the time goes in v4:
time: 94.5 us; the launch traced here: 94.2 us
  Pallas kernels  88.1 us (93%)
  other arithmetic  4.03 us (4%)
  local copies, waits for them, and re-layouts  2.08 us (2%)
    pallas_call x1, Pallas kernels, two_level_body(): pl.pallas_call(kernel, out_shape=[jax.ShapeDtypeStruct((rows, panel), F32...  88.1 us
    select_n x1, other arithmetic, two_level_body(): return jnp.where(same, jnp.float32(0.0), totals)  2.04 us

profile of v4, /device:TPU:0, one launch (start us, length us, event | category | flops | bytes accessed | tf_op | source)
XLA Modules:
  0.0 94.2 jit_solution(2584147769567524261)
XLA Ops:
  0.0 0.8 dynamic_slice.3
  0.8 1.2 %reshape.6.ids = s32[1,352]{1,0:T(1,128)} reshape(s32[352]{0:T(512)} %param.5) | data formatting | bytes 2816 | tf_op jit(solution)/shard_map/reshape | solution.py:346
  2.0 88.1 %shard_map.46 = (f32[88,352]{1,0:T(8,128)}, f32[88,352]{1,0:T(8,128)}, f32[88,704]{1,0:T(8,128)}, s32[4,1,352]{2,1,0:T(1,128)}) custom-call(bf16[2,352,2048]{2,1,0:T(8,128)(2,1)} %g.1, s32[1,352]{1,0:T(1,128)} %reshape.6.ids, f32[2]{0:T(128)} %lr_in.1, s32[2]{0:T(128)} %order_in.1), custom_call_target="tpu_custom_call" | custom-call | tf_op jit(solution)/shard_map/pallas_call | solution.py:321
  90.1 0.7 reduce
  90.8 0.1 eq.19
  90.9 1.3 %maximum_select_fusion.1 = f32[88,704]{1,0:T(8,128)S(1)} fusion(f32[88,352]{1,0:T(8,128)} %get-tuple-element.11, f32[88,352]{1,0:T(8,128)} %get-tuple-element.10, pred[]{:T(512)S(6)} %eq.22), kind=kLoop, calls=%fused_computation.2 | loop fusion | flops 185856 | bytes 495617 | tf_op jit(solution)/shard_map/jit(_where)/select_n | solution.py:349
  92.2 2.0 %fusion = f32[88,1408]{1,0:T(8,128)} fusion(f32[88,704]{1,0:T(8,128)} %get-tuple-element.12, f32[88,704]{1,0:T(8,128)S(1)} %maximum_select_fusion.1, s32[1408]{0:T(1024)S(1)} %eq.19, s32[88]{0:T(128)S(1)} %dynamic_slice.3, pred[]{:T(512)S(6)} %lt.7), kind=kLoop, calls=%fused_computation.1 | loop fusion | flops 619520 | bytes 997217 | tf_op jit(solution)/shard_map/jit(_where)/select_n | solution.py:361
